TPU v7x, 256 devices: a whole 4x4x8 slice. The times are simulated.
256 devices in a mesh: dp: 16 (over z_lo, y), tensor: 16 (over z_hi, x, core).
Axes of the slice: x: 4, y: 4, z: 8 (z_hi: 2, z_lo: 4; z = z_hi * 4 + z_lo), core: 2. Of those that a mesh axis runs over, the one named last changes fastest.
Arguments:
- activations: bfloat16 [6144, 8192], P('dp'), may hold values from -6 to 6
- out_grads: bfloat16 [6144, 16384], P('dp', 'tensor')
- left_stats: float32 [8192, 512], P('dp'), as said below
- old_roots: float32 [8192, 512], P('dp'), may hold values from -0.25 to 0.25
- refresh: int32 [4], replicated, may hold values from 0 to 15, as said below
Outputs:
- new_stats: float32 [8192, 512], P('dp')
- new_roots: float32 [8192, 512], P('dp')
- update: bfloat16 [8192, 16384], P('dp', 'tensor')
Inputs may be any that keep to these rules, and one draw needn't show every extreme that they name: `left_stats`: each block of 512 rows is symmetric with a positive diagonal. `refresh`: 4 different block numbers, always including 0 and 15.
All inputs are finite; a program needn't handle non-finite values.
Results may differ from a plain program's by a relative error of at most 0.024.
Values may be sent and summed in bfloat16 or wider, within the bound.
A program may use at most 128 MiB of HBM per device.

v0:
```python
import jax
import jax.numpy as jnp
from jax import lax
from jax.sharding import PartitionSpec as P

FF = 16384
ITERS = 6


STAT_DECAY = 0.8
TOP_PRECISION = lax.Precision.HIGHEST


def per_device(activations, out_grads, left_stats, old_roots, refresh):
    model_width = activations.shape[1]
    ff_local = out_grads.shape[1]
    dp_count = lax.axis_size("dp")
    slab_rows = model_width // dp_count
    summed = lax.psum_scatter(
        lax.dot_general(
            activations, out_grads, (((0,), (0,)), ((), ())), preferred_element_type=jnp.float32
        ).astype(jnp.bfloat16),
        "dp",
        scatter_dimension=0,
        tiled=True,
    )
    block_order = left_stats.shape[1]
    local_blocks = slab_rows // block_order
    blocks = summed.reshape(local_blocks, block_order, ff_local)
    partial_value = jnp.einsum("kbf,kcf->kbc", blocks, blocks, preferred_element_type=jnp.float32)
    summed_gram = lax.psum(partial_value.astype(jnp.bfloat16), "tensor").astype(jnp.float32)
    mix_weight = 1.0 / FF
    stat_new = (
        STAT_DECAY * left_stats.reshape(local_blocks, block_order, block_order)
        + mix_weight * summed_gram
    )
    first_block = lax.axis_index("dp") * local_blocks
    block_ids = first_block + jnp.arange(local_blocks, dtype=jnp.int32)
    refreshed = jnp.any(block_ids[:, None] == refresh[None, :], axis=1)
    old_blocks = old_roots.reshape(local_blocks, block_order, block_order)
    fro_norm = block_order * jnp.sqrt(jnp.mean(stat_new * stat_new, axis=(1, 2)) + 1e-06)
    newton_state = stat_new / fro_norm[:, None, None]
    root_scale = fro_norm ** (-0.25)
    identity = jnp.eye(block_order, dtype=jnp.float32)

    def solve_block(block_state, block_scale, block_old):
        iterate = block_scale * identity
        for loop_index in range(ITERS):
            factor = (5.0 * identity - block_state) / 4.0
            iterate = jnp.dot(iterate, factor, precision=TOP_PRECISION)
            if loop_index + 1 < ITERS:
                square = jnp.dot(factor, factor, precision=TOP_PRECISION)
                fourth = jnp.dot(square, square, precision=TOP_PRECISION)
                block_state = jnp.dot(fourth, block_state, precision=TOP_PRECISION)
        return iterate

    def keep_block(block_state, block_scale, block_old):
        return block_old

    picked = [
        lax.cond(
            refreshed[0], solve_block, keep_block, newton_state[0], root_scale[0], old_blocks[0]
        )
    ]
    new_roots = jnp.stack(picked)
    root_half = new_roots.astype(jnp.bfloat16)
    update = jnp.einsum(
        "kbc,kcf->kbf", root_half, blocks, preferred_element_type=jnp.float32
    ).astype(jnp.bfloat16)
    return (
        stat_new.reshape(slab_rows, block_order),
        new_roots.reshape(slab_rows, block_order),
        update.reshape(slab_rows, ff_local),
    )


def solution(mesh):
    placed = (P("dp", None), P("dp", "tensor"), P("dp", None), P("dp", None), P())
    return jax.shard_map(
        per_device,
        mesh=mesh,
        in_specs=placed,
        out_specs=(P("dp", None), P("dp", None), P("dp", "tensor")),
        check_vma=False,
    )
```

profile of v0, /device:TPU:1, one launch (start us, length us, event | category | flops | bytes accessed | tf_op | source)
XLA Modules:
  0.0 455.3 jit_solution(1188091479943153972)
XLA Ops:
  7.2 1.1 copy-done
  8.3 15.3 %convolution_convert_fusion = bf16[8192,1024]{1,0:T(8,128)(2,1)} fusion(bf16[384,8192]{1,0:T(8,128)(2,1)} %param.7, bf16[384,1024]{1,0:T(8,128)(2,1)S(1)} %copy-done), kind=kOutput, calls=%fused_computation.40 | convolution fusion | flops 6450839552 | bytes 23855104 | tf_op jit(solution)/shard_map/dot_general | solution.py:20
  23.7 191.1 %reduce-scatter.2.cloned.1.call-done = bf16[512,1024]{1,0:T(8,128)(2,1)} async-done(((bf16[8192,1024]{1,0:T(8,128)(2,1)}), bf16[512,1024]{1,0:T(8,128)(2,1)}) %reduce-scatter.2.cloned.1.call-update) | async-done | bytes 1048592 | tf_op jit(solution)/shard_map/reduce_scatter | solution.py:19
  214.8 3.2 fusion.34
  218.0 0.6 compare_reduce_fusion
  219.3 0.1 fusion.35
  219.4 173.0 %all-reduce.2.cloned.1.call-done = bf16[1,512,512]{2,1,0:T(8,128)(2,1)} async-done(((bf16[1,512,512]{2,1,0:T(8,128)(2,1)}), bf16[1,512,512]{2,1,0:T(8,128)(2,1)}) %all-reduce.2.cloned.1.call-update) | async-done | bytes 524304 | tf_op jit(solution)/shard_map/psum | solution.py:31
  392.4 2.5 bitcast_add_fusion
  394.9 49.9 %conditional.1 = (f32[512,512]{1,0:T(8,128)S(1)}) conditional(s32[]{:T(128)} %convert_element_type.50, (f32[512,512]{1,0:T(8,128)S(1)}) %tuple.60, (f32[1,512,512]{2,1,0:T(8,128)}, f32[512,512]{1,0:T(8,128)S(1)}, f32[512,512]{1,0:T(8,128)S(1)}, f32[512,512]{1,0:T(8,128)S(1)}, f32[512,512]{1,0:T(8,128)S(1)}, /*index=5*/f32[512,512]{1,0:T(8,128)S(1)}, ...), branch_computations={%region_3.0_spmd, %region_4.6_spmd} | conditional | flops 33833091072 | bytes 97517856 | solution.py:61
  395.5 2.2 multiply_reduce_fusion
  398.4 3.8 fusion.31
  402.2 1.8 fusion.37
  404.0 1.9 fusion.1
  405.9 2.0 fusion.7
  407.9 1.8 fusion.38
  409.8 1.9 fusion.39
  411.7 2.2 fusion.9
  413.9 1.8 fusion.40
  415.7 1.9 fusion.41
  417.6 2.0 fusion.11
  419.6 1.8 fusion.42
  421.5 1.9 fusion.43
  423.3 2.0 fusion.13
  425.4 2.1 fusion.44
  427.5 2.9 fusion
  430.4 3.3 fusion.4
  433.7 3.2 fusion.8
  437.0 1.9 fusion.10
  438.9 1.9 fusion.12
  440.8 1.9 fusion.14
  442.7 1.8 fusion.45
  444.9 3.3 convolution_convert_fusion.1
  (25 shorter events, 0.2 us)
Async XLA Ops:
  7.2 1.1 copy-start
  7.2 207.6 %reduce-scatter.2.cloned.1.call-start = ((), (), s32[]{:S(2)}) async-start(), calls=%async_computation.1 | async-start | bytes 17825792 | tf_op jit(solution)/shard_map/reduce_scatter | solution.py:19
  23.6 194.4 %copy-start.10 = (s32[4]{0:T(128)S(1)}, s32[4]{0:T(128)}, u32[]{:S(2)}) copy-start(s32[4]{0:T(128)} %param.11) | copy-start | bytes 52
  23.7 371.3 %copy-start.7 = (f32[512,512]{1,0:T(8,128)S(1)}, f32[512,512]{1,0:T(8,128)}, u32[]{:S(2)}) copy-start(f32[512,512]{1,0:T(8,128)} %param.10) | copy-start | bytes 3145732
  23.7 368.8 %all-reduce.2.cloned.1.call-start = ((), (), s32[]{:S(2)}) async-start(), calls=%async_computation.2 | async-start | bytes 1048576 | tf_op jit(solution)/shard_map/psum | solution.py:31
  395.5 8.6 %copy-start.8 = (f32[1,512,512]{2,1,0:T(8,128)S(1)}, f32[1,512,512]{2,1,0:T(8,128)}, u32[]{:S(2)}) copy-start(f32[1,512,512]{2,1,0:T(8,128)} %get-tuple-element.54) | copy-start | bytes 3145732 | tf_op jit(solution)/shard_map/cond
  405.9 8.0 %copy-start.5 = (f32[512,512]{1,0:T(8,128)}, f32[512,512]{1,0:T(8,128)S(1)}, u32[]{:S(2)}) copy-start(f32[512,512]{1,0:T(8,128)S(1)} %fusion.1) | copy-start | bytes 3145732 | tf_op jit(solution)/shard_map/cond
  417.6 7.8 %copy-start.1 = (f32[512,512]{1,0:T(8,128)}, f32[512,512]{1,0:T(8,128)S(1)}, u32[]{:S(2)}) copy-start(f32[512,512]{1,0:T(8,128)S(1)} %fusion.41) | copy-start | bytes 3145732 | tf_op jit(solution)/shard_map/cond
  423.3 4.1 copy-start.3
  430.4 8.5 %copy-start.2 = (f32[512,512]{1,0:T(8,128)S(1)}, f32[512,512]{1,0:T(8,128)}, u32[]{:S(2)}) copy-start(f32[512,512]{1,0:T(8,128)} %copy-done.1) | copy-start | bytes 3145732 | tf_op jit(solution)/shard_map/cond
  433.7 7.1 %copy-start.4 = (f32[512,512]{1,0:T(8,128)S(1)}, f32[512,512]{1,0:T(8,128)}, u32[]{:S(2)}) copy-start(f32[512,512]{1,0:T(8,128)} %copy-done.3) | copy-start | bytes 3145732 | tf_op jit(solution)/shard_map/cond
  436.9 5.8 %copy-start.9 = (f32[512,512]{1,0:T(8,128)S(1)}, f32[512,512]{1,0:T(8,128)}, u32[]{:S(2)}) copy-start(f32[512,512]{1,0:T(8,128)} %fusion) | copy-start | bytes 3145732 | tf_op jit(solution)/shard_map/cond
  444.8 3.3 copy-start.6
Sparse Core Ops, SparseCore 0:
  23.8 191.0 reduce-scatter.1
  218.1 174.2 all-reduce.1
where the time goes:
time: 460 us; the launch traced here: 455 us
  waiting for transfers between devices  364 us (79%)
  matrix products  67.7 us (15%)
  between operations  15 us (3%)
  other arithmetic  5.46 us (1%)
    reduce_scatter x1, waiting for transfers between devices, per_device(): lax.psum_scatter(lax.dot_general(activations, out_grads, (((0,), (0,)), (...  191 us
    psum x1, waiting for transfers between devices, per_device(): lax.psum(partial_value.astype(jnp.bfloat16), 'tensor').astype(jnp.float32)  173 us
    dot_general x1, matrix products, per_device(): lax.dot_general(activations, out_grads, (((0,), (0,)), ((), ())), preferr...  15.3 us
    dot_general x6, matrix products, solve_block(): iterate = jnp.dot(iterate, factor, precision=TOP_PRECISION)  14.1 us
    dot_general x5, matrix products, solve_block(): square = jnp.dot(factor, factor, precision=TOP_PRECISION)  12.1 us
    dot_general x5, matrix products, solve_block(): block_state = jnp.dot(fourth, block_state, precision=TOP_PRECISION)  10.3 us
    dot_general x5, matrix products, solve_block(): fourth = jnp.dot(square, square, precision=TOP_PRECISION)  9.45 us
  transfers between devices with their start and end apart: 2, of which 2 were waited for; matrix products, arithmetic and copies ran while one was open for 0% of the time, Pallas kernels for 0%

commit v1 on v0

v1 whole, which is shorter than its diff:
```python
import functools

import jax
import jax.numpy as jnp
from jax import lax
from jax.experimental import pallas as pl
from jax.experimental.pallas import tpu as pltpu
from jax.sharding import PartitionSpec as P

FF = 16384
ITERS = 6
STAT_DECAY = 0.8
NZ, NY, NX, NC = 4, 4, 4, 2
MESH = pl.DeviceIdType.MESH
WIDTHS = (256, 256, 256, 128, 128)
STARTS = tuple(sum(WIDTHS[:i]) for i in range(len(WIDTHS)))
ORDER = (2, 1, 3, 0)
BF16, F32 = jnp.bfloat16, jnp.float32


def _rem(a, n):
    return lax.rem(a + 2 * n, n)


def gradient_kernel(
    act, grad, red, gram_out,
    raw_near, raw_own, mine, at, gall, part, landed, own_part, gram, gsend, gcore, g1, g1land, g2, g2land,
    load_sem, az_send, az_recv, ax_send, ax_recv, ac_send, ac_recv,
    g_send, g_recv, p_send, p_recv, m_send, m_recv,
):
    tok = act.shape[0]
    blk = red.shape[0]
    row = blk // NX
    dp, tn = lax.axis_index("dp"), lax.axis_index("tensor")
    zl, y = dp // NY, lax.rem(dp, NY)
    zh, x, c = tn // (NX * NC), lax.rem(tn // NC, NX), lax.rem(tn, NC)
    z = zh * NZ + zl

    def device(dz=0, dy=0, dx=0, dc=0):
        pz = _rem(z + dz, 2 * NZ)
        return (
            lax.rem(pz, NZ) * NY + _rem(y + dy, NY),
            (pz // NZ) * NX * NC + _rem(x + dx, NX) * NC + _rem(c + dc, NC),
        )

    def remote(src, dst, send, recv, to):
        return pltpu.make_async_remote_copy(
            src_ref=src, dst_ref=dst, send_sem=send, recv_sem=recv, device_id=to, device_id_type=MESH
        )

    def arrival(dst, recv):
        return remote(dst, dst, recv, recv, device(dc=1))

    far = jnp.where(c == 0, 2, -2)
    waves = (jnp.where(c == 0, 2, 1), jnp.where(c == 0, 3, 0))
    hops = (1, -1, 2)
    near_load = []
    for w in range(2):
        for i, d in enumerate(hops):
            col = (_rem(zl + d, NZ) * NY + _rem(y + waves[w], NY)) * blk + x * row
            cp = pltpu.make_async_copy(
                act.at[:, pl.ds(pl.multiple_of(col, 128), row)], raw_near.at[w * 3 + i], load_sem.at[w * 3 + i]
            )
            cp.start()
            near_load.append(cp)
    own_load = []
    for r in range(NY):
        col = (zl * NY + _rem(y + r, NY)) * blk
        cp = pltpu.make_async_copy(act.at[:, pl.ds(pl.multiple_of(col, 128), blk)], raw_own.at[r], load_sem.at[6 + r])
        cp.start()
        own_load.append(cp)
    g_load = []
    for j, (s, wd) in enumerate(zip(STARTS, WIDTHS)):
        cp = pltpu.make_async_copy(grad.at[:, pl.ds(s, wd)], gall.at[j, pl.ds(0, tok), pl.ds(0, wd)], load_sem.at[10 + j])
        cp.start()
        g_load.append(cp)

    barrier = pltpu.get_barrier_semaphore()
    peers = [device(dz=d) for d in (1, -1, 2, -2, 4)]
    peers += [device(dy=d) for d in (1, 2, 3)] + [device(dx=d) for d in (1, 2, 3)] + [device(dc=1)]
    for p in peers:
        pl.semaphore_signal(barrier, inc=1, device_id=p, device_id_type=MESH)
    pl.semaphore_wait(barrier, len(peers))

    sent = []

    def g_slot(j, s):
        return gall.at[j, pl.ds(s * tok, tok), pl.ds(0, WIDTHS[j])]

    def g_copy(j, src, dst, way, to):
        return remote(g_slot(j, src), g_slot(j, dst), g_send.at[j, way], g_recv.at[j, dst], to)

    right, left = device(dz=1), device(dz=-1)

    def g_own(j):
        g_load[j].wait()
        pl.when(zl < NZ - 1)(lambda: g_copy(j, 0, 3, 0, right).start())
        pl.when(zl > 0)(lambda: g_copy(j, 0, 1, 1, left).start())

    def g_wait(j, s):
        arrival(g_slot(j, s), g_recv.at[j, s]).wait_recv()

    def g_relay(j):
        middle = (zl > 0) & (zl < NZ - 1)
        g_wait(j, 3)
        pl.when(middle)(lambda: g_copy(j, 3, 2, 2, right).start())
        g_wait(j, 1)
        pl.when(middle)(lambda: g_copy(j, 1, 2, 3, left).start())
        g_wait(j, 2)
        pl.when(zl == 1)(lambda: g_copy(j, 2, 3, 4, left).start())
        pl.when(zl == 2)(lambda: g_copy(j, 2, 1, 4, right).start())

    def g_drain(j):
        middle = (zl > 0) & (zl < NZ - 1)
        pl.when(zl < NZ - 1)(lambda: g_copy(j, 0, 3, 0, right).wait_send())
        pl.when(zl > 0)(lambda: g_copy(j, 0, 1, 1, left).wait_send())
        pl.when(middle)(lambda: g_copy(j, 3, 2, 2, right).wait_send())
        pl.when(middle)(lambda: g_copy(j, 1, 2, 3, left).wait_send())
        pl.when(middle)(lambda: g_copy(j, 2, 3, 4, left).wait_send())

    def at_piece(w, i, rows, count):
        slot = (-hops[i]) % NZ
        return at.at[waves[w], pl.ds(rows, count), pl.ds(slot * tok, tok)]

    my_rows = pl.multiple_of(x * row, 128)

    def a_send(w):
        for i, d in enumerate(hops):
            near_load[w * 3 + i].wait()
            mine[w * 3 + i] = raw_near[w * 3 + i].T
            cp = remote(
                mine.at[w * 3 + i], at_piece(w, i, my_rows, row), az_send.at[w * 3 + i], az_recv.at[w * 3 + i],
                device(dz=far if d == 2 else d),
            )
            cp.start()
            sent.append(cp)

    def a_share(w):
        for i in range(3):
            piece = at_piece(w, i, my_rows, row)
            arrival(piece, az_recv.at[w * 3 + i]).wait_recv()
            for k, d in enumerate((2, 1, 3)):
                cp = remote(piece, piece, ax_send.at[w * 3 + i, k], ax_recv.at[w * 3 + i, k], device(dx=d))
                cp.start()
                sent.append(cp)

    def a_core(w):
        for i in range(3):
            for k, d in enumerate((2, 1, 3)):
                rows = pl.multiple_of(_rem(x - d, NX) * row, 128)
                arrival(at_piece(w, i, rows, row), ax_recv.at[w * 3 + i, k]).wait_recv()
            piece = at_piece(w, i, 0, blk)
            cp = remote(piece, piece, ac_send.at[w * 3 + i], ac_recv.at[w * 3 + i], device(dc=1))
            cp.start()
            sent.append(cp)

    def a_wait(w):
        theirs = jnp.where(c == 0, (1, 0)[w], (2, 3)[w])
        for i in range(3):
            slot = (-hops[i]) % NZ
            arrival(at.at[theirs, pl.ds(0, blk), pl.ds(slot * tok, tok)], ac_recv.at[w * 3 + i]).wait_recv()

    def product(j, r):
        wd = WIDTHS[j]
        value = jnp.dot(at[r], gall[j, :, 0:wd], preferred_element_type=F32)
        if r == 0:
            own_part[j % 2, :, 0:wd] = value
        else:
            part[j, r - 1, :, 0:wd] = value.astype(BF16)
            cp = remote(
                part.at[j, r - 1, :, pl.ds(0, wd)], landed.at[j, NY - r - 1, :, pl.ds(0, wd)],
                p_send.at[j, r - 1], p_recv.at[j, NY - r - 1], device(dy=r),
            )
            cp.start()
            sent.append(cp)

    def finish(j):
        wd = WIDTHS[j]
        for k in (1, 0, 2):
            slot = landed.at[j, k, :, pl.ds(0, wd)]
            arrival(slot, p_recv.at[j, k]).wait_recv()
        total = own_part[j % 2, :, 0:wd] + landed[j, 0, :, 0:wd].astype(F32)
        total = total + landed[j, 1, :, 0:wd].astype(F32) + landed[j, 2, :, 0:wd].astype(F32)
        half = total.astype(BF16)
        red[:, STARTS[j]:STARTS[j] + wd] = half
        term = lax.dot_general(half, half, (((1,), (1,)), ((), ())), preferred_element_type=F32)
        if j == 0:
            gram[...] = term
        else:
            gram[...] += term

    a_send(0)
    g_own(0)
    a_send(1)
    g_own(1)
    a_share(0)
    for r in range(NY):
        own_load[r].wait()
        at[r, :, 0:tok] = raw_own[r].T
    a_share(1)
    g_relay(0)
    a_core(0)
    a_wait(0)
    product(0, 2)
    product(0, 1)
    g_own(2)
    g_relay(1)
    a_core(1)
    a_wait(1)
    product(0, 3)
    product(0, 0)
    n = len(WIDTHS)
    for j in range(1, n):
        if j + 2 < n:
            g_own(j + 2)
        if j > 1:
            g_relay(j)
        for r in ORDER:
            product(j, r)
        finish(j - 1)
    finish(n - 1)

    half_rows = blk // 2
    piece = half_rows // NX
    gsend[...] = gram[...].astype(BF16)
    other = remote(
        gsend.at[pl.ds(pl.multiple_of((1 - c) * half_rows, 128), half_rows)], gcore,
        m_send.at[0], m_recv.at[0], device(dc=1),
    )
    other.start()
    sent.append(other)
    other.wait_recv()
    mid = gram[pl.ds(pl.multiple_of(c * half_rows, 128), half_rows), :] + gcore[...].astype(F32)
    gram[0:half_rows, :] = mid
    g1[...] = mid.astype(BF16)
    for k, d in enumerate((2, 1, 3)):
        rows = pl.multiple_of(_rem(x + d, NX) * piece, 64)
        cp = remote(g1.at[pl.ds(rows, piece)], g1land.at[k], m_send.at[1 + k], m_recv.at[1 + k], device(dx=d))
        cp.start()
        sent.append(cp)
    own_rows = pl.multiple_of(x * piece, 64)
    for k in range(3):
        arrival(g1land.at[k], m_recv.at[1 + k]).wait_recv()
    low = gram[pl.ds(own_rows, piece), :]
    low = low + g1land[0].astype(F32) + g1land[1].astype(F32) + g1land[2].astype(F32)
    g2[...] = low.astype(BF16)
    cp = remote(g2, g2land, m_send.at[4], m_recv.at[4], device(dz=4))
    cp.start()
    sent.append(cp)
    cp.wait_recv()
    final_rows = pl.multiple_of(c * half_rows + x * piece, 64)
    final = gram_out.at[pl.ds(final_rows, piece)]
    gram_out[pl.ds(final_rows, piece), :] = (g2[...].astype(F32) + g2land[...].astype(F32)).astype(BF16)
    for k, d in enumerate((2, 1, 3)):
        cp = remote(final, final, m_send.at[5 + k], m_recv.at[5 + k], device(dx=d))
        cp.start()
        sent.append(cp)
    for k, d in enumerate((2, 1, 3)):
        rows = pl.multiple_of(c * half_rows + _rem(x - d, NX) * piece, 64)
        arrival(gram_out.at[pl.ds(rows, piece)], m_recv.at[5 + k]).wait_recv()
    mine_half = gram_out.at[pl.ds(pl.multiple_of(c * half_rows, 128), half_rows)]
    cp = remote(mine_half, mine_half, m_send.at[8], m_recv.at[8], device(dc=1))
    cp.start()
    sent.append(cp)
    arrival(gram_out.at[pl.ds(pl.multiple_of((1 - c) * half_rows, 128), half_rows)], m_recv.at[8]).wait_recv()

    for cp in sent:
        cp.wait_send()
    for j in range(n):
        g_drain(j)


def gradient_call(act, grad, blk):
    tok, ff = grad.shape
    n, wide = len(WIDTHS), max(WIDTHS)
    row, piece = blk // NX, blk // 2 // NX
    dma = pltpu.SemaphoreType.DMA
    flops = 2 * tok * NZ * blk * NY * ff + 2 * blk * blk * ff
    return pl.pallas_call(
        gradient_kernel,
        out_shape=(jax.ShapeDtypeStruct((blk, ff), BF16), jax.ShapeDtypeStruct((blk, blk), BF16)),
        in_specs=[pl.BlockSpec(memory_space=pl.ANY)] * 2,
        out_specs=[pl.BlockSpec(memory_space=pltpu.VMEM)] * 2,
        scratch_shapes=[
            pltpu.VMEM((6, tok, row), BF16),
            pltpu.VMEM((NY, tok, blk), BF16),
            pltpu.VMEM((6, row, tok), BF16),
            pltpu.VMEM((NY, blk, NZ * tok), BF16),
            pltpu.VMEM((n, NZ * tok, wide), BF16),
            pltpu.VMEM((n, NY - 1, blk, wide), BF16),
            pltpu.VMEM((n, NY - 1, blk, wide), BF16),
            pltpu.VMEM((2, blk, wide), F32),
            pltpu.VMEM((blk, blk), F32),
            pltpu.VMEM((blk, blk), BF16),
            pltpu.VMEM((blk // 2, blk), BF16),
            pltpu.VMEM((blk // 2, blk), BF16),
            pltpu.VMEM((3, piece, blk), BF16),
            pltpu.VMEM((piece, blk), BF16),
            pltpu.VMEM((piece, blk), BF16),
            dma((10 + n,)), dma((6,)), dma((6,)), dma((6, 3)), dma((6, 3)), dma((6,)), dma((6,)),
            dma((n, 5)), dma((n, 4)), dma((n, 3)), dma((n, 3)), dma((9,)), dma((9,)),
        ],
        compiler_params=pltpu.CompilerParams(
            collective_id=0, has_side_effects=True, vmem_limit_bytes=56 * 2**20
        ),
        cost_estimate=pl.CostEstimate(flops=flops, bytes_accessed=8 * 2**20, transcendentals=0),
        name="gradient",
    )(act, grad)


def _mm(a, b):
    return jnp.dot(a.astype(BF16), b.astype(BF16), preferred_element_type=F32)


def root_kernel(refresh, gram, left, old, red, stats, roots, update, state, root, square):
    blk = gram.shape[0]
    me = lax.axis_index("dp")
    new = STAT_DECAY * left[...] + (1.0 / FF) * gram[...].astype(F32)
    stats[...] = new
    picked = refresh[0] == me
    for i in range(1, refresh.shape[0]):
        picked = picked | (refresh[i] == me)

    @pl.when(picked)
    def _():
        value = stats[...]
        norm = blk * jnp.sqrt(jnp.mean(value * value, keepdims=True) + 1e-6)
        scale = jnp.exp(-0.25 * jnp.log(norm))
        state[...] = value * (0.25 / norm)
        eye = (
            lax.broadcasted_iota(jnp.int32, (blk, blk), 0) == lax.broadcasted_iota(jnp.int32, (blk, blk), 1)
        ).astype(F32)
        root[...] = scale * (1.25 * eye - state[...])
        for i in range(ITERS - 1):
            half = state[...].astype(BF16)
            square[...] = jnp.dot(half, half, preferred_element_type=F32)
            cube = jnp.dot(half, square[...].astype(BF16), preferred_element_type=F32)
            cube = 9.375 * state[...] - 5.0 * square[...] + cube
            last = _mm(square[...], cube)
            state[...] = 2.44140625 * state[...] - 7.8125 * square[...] + last
            root[...] = 1.25 * root[...] - _mm(root[...], state[...])
        roots[...] = root[...]

    @pl.when(jnp.logical_not(picked))
    def _():
        roots[...] = old[...]

    update[...] = jnp.dot(roots[...].astype(BF16), red[...], preferred_element_type=F32).astype(BF16)


def root_call(refresh, gram, left, old, red):
    blk, ff = red.shape
    vmem = pl.BlockSpec(memory_space=pltpu.VMEM)
    return pl.pallas_call(
        root_kernel,
        out_shape=(
            jax.ShapeDtypeStruct((blk, blk), F32),
            jax.ShapeDtypeStruct((blk, blk), F32),
            jax.ShapeDtypeStruct((blk, ff), BF16),
        ),
        in_specs=[pl.BlockSpec(memory_space=pltpu.SMEM)] + [vmem] * 4,
        out_specs=[vmem] * 3,
        scratch_shapes=[pltpu.VMEM((blk, blk), F32)] * 3,
        compiler_params=pltpu.CompilerParams(vmem_limit_bytes=40 * 2**20),
        name="root",
    )(refresh, gram, left, old, red)


def per_device(activations, out_grads, left_stats, old_roots, refresh):
    reduced, gram = gradient_call(activations, out_grads, left_stats.shape[1])
    return root_call(refresh, gram, left_stats, old_roots, reduced)


def solution(mesh):
    placed = (P("dp", None), P("dp", "tensor"), P("dp", None), P("dp", None), P())
    return jax.shard_map(
        per_device,
        mesh=mesh,
        in_specs=placed,
        out_specs=(P("dp", None), P("dp", None), P("dp", "tensor")),
        check_vma=False,
    )
```

time: 460 us -> 132 us (0.29)
  waiting for transfers between devices: 364 us -> 0 us
  Pallas kernels: 0 us -> 129 us
  matrix products: 67.7 us -> 0 us
  between operations: 15 us -> 0.7 us
  other arithmetic: 5.46 us -> 0 us
    reduce_scatter x1 -> x0, waiting for transfers between devices: 191 us -> none  [per_device(): lax.psum_scatter(lax.dot_general(activations, out_grads, (((0,), (0,)), (...]
    psum x1 -> x0, waiting for transfers between devices: 173 us -> none  [per_device(): lax.psum(partial_value.astype(jnp.bfloat16), 'tensor').astype(jnp.float32)]
    pallas_call x0 -> x2, Pallas kernels: none -> 129 us  [the longest x1 119 us: gradient_call(): pl.pallas_call(gradient_kernel, out_shape=(jax.ShapeDtypeStruct((blk, ff)...]
    dot_general x24 -> x0, matrix products: 67.7 us -> none  [the longest x1 15.3 us: per_device(): lax.dot_general(activations, out_grads, (((0,), (0,)), ((), ())), preferr...]
  transfers between devices with their start and end apart: 2 -> 0, of which waited for: 2 -> 0; matrix products, arithmetic and copies ran while one was open for 0% -> 0% of each run, Pallas kernels for 0% -> 0%
where the time goes in v1:
time: 132 us
  Pallas kernels  129 us (98%)
  local copies, waits for them, and re-layouts  2.27 us (2%)
    pallas_call x1, Pallas kernels, gradient_call(): pl.pallas_call(gradient_kernel, out_shape=(jax.ShapeDtypeStruct((blk, ff)...  119 us
    pallas_call x1, Pallas kernels, root_call(): pl.pallas_call(root_kernel, out_shape=(jax.ShapeDtypeStruct((blk, blk), F...  10 us

profile of v1, /device:TPU:1, one launch (start us, length us, event | category | flops | bytes accessed | tf_op | source)
XLA Modules:
  0.0 131.5 jit_solution(12042944189464082556)
XLA Ops:
  0.6 0.0 copy-start.4
  0.6 0.0 copy-start.1
  0.7 0.0 copy-start
  0.7 118.5 %gradient.1 = (bf16[512,1024]{1,0:T(8,128)(2,1)}, bf16[512,512]{1,0:T(8,128)(2,1)}) custom-call(bf16[384,8192]{1,0:T(8,128)(2,1)} %act.1, bf16[384,1024]{1,0:T(8,128)(2,1)} %grad.1), custom_call_target="tpu_custom_call" | custom-call | flops 6979321856 | bytes 8388608 | tf_op jit(solution)/shard_map/gradient/pallas_call | solution.py:279
  119.2 0.0 copy-done.4
  119.2 0.0 copy-done.1
  119.2 0.0 copy-done
  119.2 0.0 copy-start.2
  119.2 1.2 copy-done.2
  120.4 0.0 copy-start.3
  120.4 1.0 copy-done.3
  121.5 10.0 %root.1 = (f32[512,512]{1,0:T(8,128)}, f32[512,512]{1,0:T(8,128)}, bf16[512,1024]{1,0:T(8,128)(2,1)}) custom-call(s32[4]{0:T(128)S(1)} %copy-done.4, bf16[512,512]{1,0:T(8,128)(2,1)S(1)} %copy-done.3, f32[512,512]{1,0:T(8,128)S(1)} %copy-done, f32[512,512]{1,0:T(8,128)S(1)} %copy-done.1, bf16[512,1024]{1,0:T(8,128)(2,1)S(1)} %copy-done.2), custom_call_target="tpu_custom_call" | custom-call | tf_op jit(solution)/shard_map/root/pallas_call | solution.py:354
Async XLA Ops:
  0.6 118.6 %copy-start.4 = (s32[4]{0:T(128)S(1)}, s32[4]{0:T(128)}, u32[]{:S(2)}) copy-start(s32[4]{0:T(128)} %refresh.1) | copy-start | bytes 52
  0.6 118.6 %copy-start.1 = (f32[512,512]{1,0:T(8,128)S(1)}, f32[512,512]{1,0:T(8,128)}, u32[]{:S(2)}) copy-start(f32[512,512]{1,0:T(8,128)} %old.1) | copy-start | bytes 3145732
  0.7 118.6 %copy-start = (f32[512,512]{1,0:T(8,128)S(1)}, f32[512,512]{1,0:T(8,128)}, u32[]{:S(2)}) copy-start(f32[512,512]{1,0:T(8,128)} %left.1) | copy-start | bytes 3145732
  119.2 1.2 copy-start.2
  120.4 1.0 copy-start.3

commit v2 on v1

v2 whole, which is shorter than its diff:
```python
import functools

import jax
import jax.numpy as jnp
from jax import lax
from jax.experimental import pallas as pl
from jax.experimental.pallas import tpu as pltpu
from jax.sharding import PartitionSpec as P

FF = 16384
ITERS = 6
STAT_DECAY = 0.8
NZ, NY, NX, NC = 4, 4, 4, 2
MESH = pl.DeviceIdType.MESH
WIDTHS = (128, 128, 128, 128, 128, 128, 128, 128)
STARTS = tuple(sum(WIDTHS[:i]) for i in range(len(WIDTHS)))
Z_FIRST = (False, True, False, True, False, False, True, False)
DIRECT = ()
ORDER = (3, 2, 1, 0)
OWN, KEPT = len(WIDTHS), len(WIDTHS)
TILE = 128
PAIRS = tuple((i, j) for i in range(4) for j in range(i + 1))
BF16, F32 = jnp.bfloat16, jnp.float32


def _rem(a, n):
    return lax.rem(a + 2 * n, n)


def gradient_kernel(
    act, grad, red, gram_out,
    raw_near, raw_own, mine, at, gall, part, land, kept, own_part,
    gram, gram_half, gsend, gcore, g1, g1land, g2, g2land,
    load_sem, az_send, az_recv, ax_send, ax_recv, ac_send, ac_recv,
    g_send, g_recv, p_send, p_recv, m_send, m_recv,
):
    tok = act.shape[0]
    blk = red.shape[0]
    row = blk // NX
    share = row // NC
    dp, tn = lax.axis_index("dp"), lax.axis_index("tensor")
    zl, y = dp // NY, lax.rem(dp, NY)
    zh, x, c = tn // (NX * NC), lax.rem(tn // NC, NX), lax.rem(tn, NC)
    z = zh * NZ + zl

    def device(dz=0, dy=0, dx=0, dc=0):
        pz = _rem(z + dz, 2 * NZ)
        return (
            lax.rem(pz, NZ) * NY + _rem(y + dy, NY),
            (pz // NZ) * NX * NC + _rem(x + dx, NX) * NC + _rem(c + dc, NC),
        )

    def remote(src, dst, send, recv, to):
        return pltpu.make_async_remote_copy(
            src_ref=src, dst_ref=dst, send_sem=send, recv_sem=recv, device_id=to, device_id_type=MESH
        )

    def arrival(dst, recv):
        return remote(dst, dst, recv, recv, device(dc=1))

    far = jnp.where(c == 0, 2, -2)
    line = jnp.where(zl < 2, 2, -2)
    near = 1 - 2 * lax.rem(zl, 2)
    even_y = 1 - 2 * lax.rem(y, 2)
    back_y = NY - 1 - 2 * y

    def row_block(dz2, dy1, r):
        rz = _rem(zl + 2 * dz2, NZ)
        ry = y + even_y * dy1
        rz = rz + (1 - 2 * lax.rem(rz, 2)) * (r % 2)
        ry = ry + (NY - 1 - 2 * ry) * (r // 2)
        return rz * NY + ry

    sources = ((1, 0), (0, 1), (1, 1))
    near_load = {}
    for r in ORDER:
        for i, (dz2, dy1) in enumerate(sources):
            col = row_block(dz2, dy1, r) * blk + x * row
            cp = pltpu.make_async_copy(
                act.at[:, pl.ds(pl.multiple_of(col, 128), row)], raw_near.at[r * 3 + i], load_sem.at[r * 3 + i]
            )
            cp.start()
            near_load[r, i] = cp
    own_load = []
    for r in range(NY):
        col = row_block(0, 0, r) * blk
        cp = pltpu.make_async_copy(act.at[:, pl.ds(pl.multiple_of(col, 128), blk)], raw_own.at[r], load_sem.at[12 + r])
        cp.start()
        own_load.append(cp)
    g_load = []
    for j, (s, wd) in enumerate(zip(STARTS, WIDTHS)):
        cp = pltpu.make_async_copy(grad.at[:, pl.ds(s, wd)], gall.at[j, pl.ds(0, tok), pl.ds(0, wd)], load_sem.at[16 + j])
        cp.start()
        g_load.append(cp)

    barrier = pltpu.get_barrier_semaphore()
    peers = [device(dz=d) for d in (2, -2, 4)] + [device(dz=d, dy=even_y) for d in (2, -2)]
    peers += [device(dz=near), device(dy=even_y), device(dy=back_y), device(dz=near, dy=back_y)]
    peers += [device(dx=d) for d in (1, 2, 3)] + [device(dc=1)]
    for p in peers:
        pl.semaphore_signal(barrier, inc=1, device_id=p, device_id_type=MESH)
    pl.semaphore_wait(barrier, len(peers))

    sent = []

    def g_copy(j, src, dst, to):
        cols = pl.ds(0, WIDTHS[j])
        cp = remote(
            gall.at[j, pl.ds(src * tok, tok), cols], gall.at[j, pl.ds(dst * tok, tok), cols],
            g_send.at[j, dst], g_recv.at[j, dst], to,
        )
        cp.start()
        sent.append(cp)

    def g_own(j):
        g_load[j].wait()
        g_copy(j, 0, 1, device(dz=line))
        g_copy(j, 0, 2, device(dy=even_y))

    def g_wait(j, slot):
        arrival(gall.at[j, pl.ds(slot * tok, tok), pl.ds(0, WIDTHS[j])], g_recv.at[j, slot]).wait_recv()

    def g_pass(j):
        g_wait(j, 1)
        g_copy(j, 1, 3, device(dy=even_y))

    def g_rest(j):
        g_wait(j, 2)
        g_wait(j, 3)

    def columns(i):
        return pl.ds((i + 1) * tok, tok)

    def a_send(r):
        for i, (dz2, dy1) in enumerate(sources):
            near_load[r, i].wait()
            mine[r * 3 + i] = raw_near[r * 3 + i].T
            cp = remote(
                mine.at[r * 3 + i, pl.ds(pl.multiple_of(c * share, share), share)], at.at[r, x, c, :, columns(i)],
                az_send.at[r * 3 + i], az_recv.at[r * 3 + i], device(dz=far * dz2, dy=even_y * dy1),
            )
            cp.start()
            sent.append(cp)

    def a_share(r):
        for i in range(3):
            piece = at.at[r, x, c, :, columns(i)]
            arrival(piece, az_recv.at[r * 3 + i]).wait_recv()
            for k, d in enumerate((1, -1)):
                cp = remote(piece, piece, ax_send.at[r * 3 + i, k], ax_recv.at[r * 3 + i, k], device(dx=d))
                cp.start()
                sent.append(cp)

    def a_relay(r):
        for i in range(3):
            for k, d in enumerate((1, -1)):
                origin = _rem(x - d, NX)
                arrival(at.at[r, origin, c, :, columns(i)], ax_recv.at[r * 3 + i, k]).wait_recv()
                piece = at.at[r, origin, c, pl.ds(k * (share // 2), share // 2), columns(i)]
                cp = remote(piece, piece, ax_send.at[r * 3 + i, 2 + k], ax_recv.at[r * 3 + i, 2 + k], device(dx=d))
                cp.start()
                sent.append(cp)

    def a_core(r):
        origin = _rem(x + 2, NX)
        for i in range(3):
            for k in range(2):
                piece = at.at[r, origin, c, pl.ds(k * (share // 2), share // 2), columns(i)]
                arrival(piece, ax_recv.at[r * 3 + i, 2 + k]).wait_recv()
        piece = at.at[r, :, c, :, pl.ds(tok, 3 * tok)]
        cp = remote(piece, piece, ac_send.at[r], ac_recv.at[r], device(dc=1))
        cp.start()
        sent.append(cp)

    def a_wait(r):
        arrival(at.at[r, :, 1 - c, :, pl.ds(tok, 3 * tok)], ac_recv.at[r]).wait_recv()

    def first(j):
        return device(dz=near) if Z_FIRST[j] else device(dy=back_y)

    def second(j):
        return device(dy=back_y) if Z_FIRST[j] else device(dz=near)

    def p_copy(j, k, to):
        cols = pl.ds(0, WIDTHS[j])
        cp = remote(part.at[j, k, :, cols], land.at[j, k, :, cols], p_send.at[j, k], p_recv.at[j, k], to)
        cp.start()
        sent.append(cp)

    def p_wait(j, k):
        arrival(land.at[j, k, :, pl.ds(0, WIDTHS[j])], p_recv.at[j, k]).wait_recv()

    def product(j, r):
        wd = WIDTHS[j]
        value = jnp.dot(at[r].reshape(blk, NZ * tok), gall[j, :, 0:wd], preferred_element_type=F32)
        if j in DIRECT and r > 0:
            part[j, r - 1, :, 0:wd] = value.astype(BF16)
            p_copy(j, r - 1, device(dz=near * (r % 2), dy=back_y * (r // 2)))
        elif r == 0:
            own_part[j % OWN, :, 0:wd] = value
        elif r == (2 if Z_FIRST[j] else 1):
            kept[j % KEPT, :, 0:wd] = value
        else:
            k = 0 if r == 3 else 1
            part[j, k, :, 0:wd] = value.astype(BF16)
            p_copy(j, k, first(j))

    def p_pass(j):
        wd = WIDTHS[j]
        p_wait(j, 0)
        part[j, 2, :, 0:wd] = (kept[j % KEPT, :, 0:wd] + land[j, 0, :, 0:wd].astype(F32)).astype(BF16)
        p_copy(j, 2, second(j))

    def finish(j):
        wd = WIDTHS[j]
        p_wait(j, 1)
        p_wait(j, 2)
        total = own_part[j % OWN, :, 0:wd]
        if j in DIRECT:
            p_wait(j, 0)
            total = total + land[j, 0, :, 0:wd].astype(F32)
        total = total + land[j, 1, :, 0:wd].astype(F32) + land[j, 2, :, 0:wd].astype(F32)
        red[:, STARTS[j]:STARTS[j] + wd] = total.astype(BF16)
        half = red[:, STARTS[j]:STARTS[j] + wd]
        for i in range(blk // TILE):
            term = lax.dot_general(
                half[i * TILE:(i + 1) * TILE], half[:(i + 1) * TILE], (((1,), (1,)), ((), ())), preferred_element_type=F32
            )
            for k in range(i + 1):
                at_row = PAIRS.index((i, k)) * TILE
                tile = term[:, k * TILE:(k + 1) * TILE]
                if j == 0:
                    gram[at_row:at_row + TILE] = tile
                else:
                    gram[at_row:at_row + TILE] += tile

    def turn_own(r):
        own_load[r].wait()
        at[r, :, :, :, 0:tok] = raw_own[r].T.reshape(NX, NC, share, tok)

    n = len(WIDTHS)
    a_send(3)
    a_send(2)
    a_send(1)
    a_send(0)
    g_own(0)
    g_own(1)
    g_own(2)
    g_own(3)
    turn_own(3)
    turn_own(2)
    turn_own(1)
    turn_own(0)
    a_share(3)
    a_share(2)
    a_share(1)
    a_relay(3)
    a_share(0)
    a_relay(2)
    g_pass(0)
    g_own(4)
    a_relay(1)
    a_core(3)
    g_pass(1)
    g_own(5)
    g_rest(0)
    a_wait(3)
    product(0, 3)
    a_relay(0)
    g_pass(2)
    g_own(6)
    a_core(2)
    g_rest(1)
    product(1, 3)
    a_core(1)
    a_wait(2)
    product(0, 2)
    product(1, 2)
    a_core(0)
    g_pass(3)
    g_own(7)
    a_wait(1)
    product(0, 1)
    p_pass(0)
    product(1, 1)
    g_rest(2)
    product(2, 3)
    product(2, 2)
    product(2, 1)
    a_wait(0)
    product(0, 0)
    product(1, 0)
    p_pass(1)
    product(2, 0)
    g_pass(4)
    g_rest(3)
    product(3, 3)
    product(3, 1)
    product(3, 2)
    product(3, 0)
    p_pass(2)
    finish(0)
    g_pass(5)
    g_rest(4)
    product(4, 3)
    product(4, 2)
    product(4, 1)
    product(4, 0)
    finish(1)
    g_pass(6)
    g_rest(5)
    product(5, 3)
    product(5, 2)
    p_pass(3)
    product(5, 1)
    product(5, 0)
    p_pass(4)
    g_pass(7)
    g_rest(6)
    product(6, 3)
    product(6, 1)
    product(6, 2)
    product(6, 0)
    finish(2)
    p_pass(5)
    g_rest(7)
    product(7, 3)
    product(7, 2)
    product(7, 1)
    product(7, 0)
    finish(4)
    p_pass(6)
    finish(3)
    p_pass(7)
    finish(5)
    finish(7)
    finish(6)

    half_rows = gram.shape[0] // 2
    piece = half_rows // NX
    gsend[...] = gram[...].astype(BF16)
    other = remote(
        gsend.at[pl.ds(pl.multiple_of((1 - c) * half_rows, 128), half_rows)], gcore,
        m_send.at[0], m_recv.at[0], device(dc=1),
    )
    other.start()
    sent.append(other)
    other.wait_recv()
    mid = gram[pl.ds(pl.multiple_of(c * half_rows, 128), half_rows), :] + gcore[...].astype(F32)
    gram[0:half_rows, :] = mid
    g1[...] = mid.astype(BF16)
    for k, d in enumerate((2, 1, 3)):
        rows = pl.multiple_of(_rem(x + d, NX) * piece, 32)
        cp = remote(g1.at[pl.ds(rows, piece)], g1land.at[k], m_send.at[1 + k], m_recv.at[1 + k], device(dx=d))
        cp.start()
        sent.append(cp)
    own_rows = pl.multiple_of(x * piece, 32)
    for k in range(3):
        arrival(g1land.at[k], m_recv.at[1 + k]).wait_recv()
    low = gram[pl.ds(own_rows, piece), :]
    low = low + g1land[0].astype(F32) + g1land[1].astype(F32) + g1land[2].astype(F32)
    g2[...] = low.astype(BF16)
    cp = remote(g2, g2land, m_send.at[4], m_recv.at[4], device(dz=4))
    cp.start()
    sent.append(cp)
    cp.wait_recv()
    final_rows = pl.multiple_of(c * half_rows + x * piece, 32)
    final = gram_half.at[pl.ds(final_rows, piece)]
    gram_half[pl.ds(final_rows, piece), :] = (g2[...].astype(F32) + g2land[...].astype(F32)).astype(BF16)
    for k, d in enumerate((2, 1, 3)):
        cp = remote(final, final, m_send.at[5 + k], m_recv.at[5 + k], device(dx=d))
        cp.start()
        sent.append(cp)
    for k, d in enumerate((2, 1, 3)):
        rows = pl.multiple_of(c * half_rows + _rem(x - d, NX) * piece, 32)
        arrival(gram_half.at[pl.ds(rows, piece)], m_recv.at[5 + k]).wait_recv()
    mine_half = gram_half.at[pl.ds(pl.multiple_of(c * half_rows, 128), half_rows)]
    cp = remote(mine_half, mine_half, m_send.at[8], m_recv.at[8], device(dc=1))
    cp.start()
    sent.append(cp)
    arrival(gram_half.at[pl.ds(pl.multiple_of((1 - c) * half_rows, 128), half_rows)], m_recv.at[8]).wait_recv()

    gram_out[...] = gram_half[...]

    for cp in sent:
        cp.wait_send()


def gradient_call(act, grad, blk):
    tok, ff = grad.shape
    n, wide = len(WIDTHS), max(WIDTHS)
    row = blk // NX
    packed = len(PAIRS) * TILE
    dma = pltpu.SemaphoreType.DMA
    flops = 2 * tok * NZ * blk * NY * ff + 2 * blk * blk * ff
    return pl.pallas_call(
        gradient_kernel,
        out_shape=(pltpu.VMEM((blk, ff), BF16), pltpu.VMEM((packed, TILE), BF16)),
        in_specs=[pl.BlockSpec(memory_space=pl.ANY)] * 2,
        out_specs=[pl.BlockSpec(memory_space=pltpu.VMEM)] * 2,
        scratch_shapes=[
            pltpu.VMEM((12, tok, row), BF16),
            pltpu.VMEM((NY, tok, blk), BF16),
            pltpu.VMEM((12, row, tok), BF16),
            pltpu.VMEM((NY, NX, NC, row // NC, NZ * tok), BF16),
            pltpu.VMEM((n, NZ * tok, wide), BF16),
            pltpu.VMEM((n, 3, blk, wide), BF16),
            pltpu.VMEM((n, 3, blk, wide), BF16),
            pltpu.VMEM((KEPT, blk, wide), F32),
            pltpu.VMEM((OWN, blk, wide), F32),
            pltpu.VMEM((packed, TILE), F32),
            pltpu.VMEM((packed, TILE), BF16),
            pltpu.VMEM((packed, TILE), BF16),
            pltpu.VMEM((packed // 2, TILE), BF16),
            pltpu.VMEM((packed // 2, TILE), BF16),
            pltpu.VMEM((3, packed // 8, TILE), BF16),
            pltpu.VMEM((packed // 8, TILE), BF16),
            pltpu.VMEM((packed // 8, TILE), BF16),
            dma((16 + n,)), dma((12,)), dma((12,)), dma((12, 4)), dma((12, 4)), dma((NY,)), dma((NY,)),
            dma((n, 4)), dma((n, 4)), dma((n, 3)), dma((n, 3)), dma((9,)), dma((9,)),
        ],
        compiler_params=pltpu.CompilerParams(
            collective_id=0, has_side_effects=True, vmem_limit_bytes=56 * 2**20
        ),
        cost_estimate=pl.CostEstimate(flops=flops, bytes_accessed=8 * 2**20, transcendentals=0),
        name="gradient",
    )(act, grad)


def _mm(a, b):
    return jnp.dot(a.astype(BF16), b.astype(BF16), preferred_element_type=F32)


def root_kernel(refresh, gram, left, old, red, stats, roots, update, state, root, square):
    blk = left.shape[0]
    me = lax.axis_index("dp")
    for k, (i, j) in enumerate(PAIRS):
        term = (1.0 / FF) * gram[k * TILE:(k + 1) * TILE].astype(F32)
        rows, cols = slice(i * TILE, (i + 1) * TILE), slice(j * TILE, (j + 1) * TILE)
        stats[rows, cols] = STAT_DECAY * left[rows, cols] + term
        if i != j:
            stats[cols, rows] = STAT_DECAY * left[cols, rows] + term.T
    picked = refresh[0] == me
    for i in range(1, refresh.shape[0]):
        picked = picked | (refresh[i] == me)

    @pl.when(picked)
    def _():
        value = stats[...]
        norm = blk * jnp.sqrt(jnp.mean(value * value, keepdims=True) + 1e-6)
        scale = jnp.exp(-0.25 * jnp.log(norm))
        state[...] = value * (0.25 / norm)
        eye = (
            lax.broadcasted_iota(jnp.int32, (blk, blk), 0) == lax.broadcasted_iota(jnp.int32, (blk, blk), 1)
        ).astype(F32)
        root[...] = scale * (1.25 * eye - state[...])
        for i in range(ITERS - 1):
            half = state[...].astype(BF16)
            square[...] = jnp.dot(half, half, preferred_element_type=F32)
            cube = jnp.dot(half, square[...].astype(BF16), preferred_element_type=F32)
            cube = 9.375 * state[...] - 5.0 * square[...] + cube
            last = _mm(square[...], cube)
            state[...] = 2.44140625 * state[...] - 7.8125 * square[...] + last
            root[...] = 1.25 * root[...] - _mm(root[...], state[...])
        roots[...] = root[...]

    @pl.when(jnp.logical_not(picked))
    def _():
        roots[...] = old[...]

    update[...] = jnp.dot(roots[...].astype(BF16), red[...], preferred_element_type=F32).astype(BF16)


def root_call(refresh, gram, left, old, red):
    blk, ff = red.shape
    vmem = pl.BlockSpec(memory_space=pltpu.VMEM)
    return pl.pallas_call(
        root_kernel,
        out_shape=(
            jax.ShapeDtypeStruct((blk, blk), F32),
            jax.ShapeDtypeStruct((blk, blk), F32),
            jax.ShapeDtypeStruct((blk, ff), BF16),
        ),
        in_specs=[pl.BlockSpec(memory_space=pltpu.SMEM)] + [vmem] * 4,
        out_specs=[vmem] * 3,
        scratch_shapes=[pltpu.VMEM((blk, blk), F32)] * 3,
        compiler_params=pltpu.CompilerParams(vmem_limit_bytes=40 * 2**20),
        name="root",
    )(refresh, gram, left, old, red)


def per_device(activations, out_grads, left_stats, old_roots, refresh):
    reduced, gram = gradient_call(activations, out_grads, left_stats.shape[1])
    return root_call(refresh, gram, left_stats, old_roots, reduced)


def solution(mesh):
    placed = (P("dp", None), P("dp", "tensor"), P("dp", None), P("dp", None), P())
    return jax.shard_map(
        per_device,
        mesh=mesh,
        in_specs=placed,
        out_specs=(P("dp", None), P("dp", None), P("dp", "tensor")),
        check_vma=False,
    )
```

time: 132 us -> 111 us (0.84)
  Pallas kernels: 129 us -> 109 us
  local copies, waits for them, and re-layouts: 2.27 us -> 0.01 us
    pallas_call x1, Pallas kernels: 119 us -> 98.8 us  [gradient_call(): pl.pallas_call(gradient_kernel, out_shape=(pltpu.VMEM((blk, ff), BF16), p...]
    unnamed x10 -> x6, local copies, waits for them, and re-layouts: 2.27 us -> 0.01 us
where the time goes in v2:
time: 111 us; the launch traced here: 109 us
  Pallas kernels  109 us (98%)
    pallas_call x1, Pallas kernels, gradient_call(): pl.pallas_call(gradient_kernel, out_shape=(pltpu.VMEM((blk, ff), BF16), p...  98.8 us
    pallas_call x1, Pallas kernels, root_call(): pl.pallas_call(root_kernel, out_shape=(jax.ShapeDtypeStruct((blk, blk), F...  9.9 us

profile of v2, /device:TPU:1, one launch (start us, length us, event | category | flops | bytes accessed | tf_op | source)
XLA Modules:
  0.0 109.4 jit_solution(6757361026724544586)
XLA Ops:
  0.6 0.0 copy-start.2
  0.6 0.0 copy-start.1
  0.7 0.0 copy-start
  0.7 98.8 %gradient.1 = (bf16[512,1024]{1,0:T(8,128)(2,1)S(1)}, bf16[1280,128]{1,0:T(8,128)(2,1)S(1)}) custom-call(bf16[384,8192]{1,0:T(8,128)(2,1)} %act.1, bf16[384,1024]{1,0:T(8,128)(2,1)} %grad.1), custom_call_target="tpu_custom_call" | custom-call | flops 6979321856 | bytes 8388608 | tf_op jit(solution)/shard_map/gradient/pallas_call | solution.py:396
  99.5 0.0 copy-done.2
  99.5 0.0 copy-done.1
  99.5 0.0 copy-done
  99.5 9.9 %root.1 = (f32[512,512]{1,0:T(8,128)}, f32[512,512]{1,0:T(8,128)}, bf16[512,1024]{1,0:T(8,128)(2,1)}) custom-call(s32[4]{0:T(128)S(1)} %copy-done.2, bf16[1280,128]{1,0:T(8,128)(2,1)S(1)} %get-tuple-element.5.gram, f32[512,512]{1,0:T(8,128)S(1)} %copy-done, f32[512,512]{1,0:T(8,128)S(1)} %copy-done.1, bf16[512,1024]{1,0:T(8,128)(2,1)S(1)} %get-tuple-element.6.red), custom_call_target="tpu_custom_call" | custom-call | tf_op jit(solution)/shard_map/root/pallas_call | solution.py:477
Async XLA Ops:
  0.6 98.9 %copy-start.2 = (s32[4]{0:T(128)S(1)}, s32[4]{0:T(128)}, u32[]{:S(2)}) copy-start(s32[4]{0:T(128)} %refresh.1) | copy-start | bytes 52
  0.6 98.9 %copy-start.1 = (f32[512,512]{1,0:T(8,128)S(1)}, f32[512,512]{1,0:T(8,128)}, u32[]{:S(2)}) copy-start(f32[512,512]{1,0:T(8,128)} %old.1) | copy-start | bytes 3145732
  0.7 98.9 %copy-start = (f32[512,512]{1,0:T(8,128)S(1)}, f32[512,512]{1,0:T(8,128)}, u32[]{:S(2)}) copy-start(f32[512,512]{1,0:T(8,128)} %left.1) | copy-start | bytes 3145732

commit v3 on v2

--- a/solution.py
+++ b/solution.py
@@ -14,10 +14,9 @@
 MESH = pl.DeviceIdType.MESH
 WIDTHS = (128, 128, 128, 128, 128, 128, 128, 128)
 STARTS = tuple(sum(WIDTHS[:i]) for i in range(len(WIDTHS)))
-Z_FIRST = (False, True, False, True, False, False, True, False)
-DIRECT = ()
+SPLIT = 384
+X_DIRECT = ()
 ORDER = (3, 2, 1, 0)
-OWN, KEPT = len(WIDTHS), len(WIDTHS)
 TILE = 128
 PAIRS = tuple((i, j) for i in range(4) for j in range(i + 1))
 BF16, F32 = jnp.bfloat16, jnp.float32
@@ -29,7 +28,7 @@
 
 def gradient_kernel(
     act, grad, red, gram_out,
-    raw_near, raw_own, mine, at, gall, part, land, kept, own_part,
+    raw_near, raw_own, mine, at, gall, part, fwd, land, kept, own_part,
     gram, gram_half, gsend, gcore, g1, g1land, g2, g2land,
     load_sem, az_send, az_recv, ax_send, ax_recv, ac_send, ac_recv,
     g_send, g_recv, p_send, p_recv, m_send, m_recv,
@@ -95,7 +94,7 @@
 
     barrier = pltpu.get_barrier_semaphore()
     peers = [device(dz=d) for d in (2, -2, 4)] + [device(dz=d, dy=even_y) for d in (2, -2)]
-    peers += [device(dz=near), device(dy=even_y), device(dy=back_y), device(dz=near, dy=back_y)]
+    peers += [device(dz=near), device(dy=even_y), device(dy=back_y)]
     peers += [device(dx=d) for d in (1, 2, 3)] + [device(dc=1)]
     for p in peers:
         pl.semaphore_signal(barrier, inc=1, device_id=p, device_id_type=MESH)
@@ -142,28 +141,31 @@
             cp.start()
             sent.append(cp)
 
-    def a_share(r):
-        for i in range(3):
-            piece = at.at[r, x, c, :, columns(i)]
-            arrival(piece, az_recv.at[r * 3 + i]).wait_recv()
-            for k, d in enumerate((1, -1)):
-                cp = remote(piece, piece, ax_send.at[r * 3 + i, k], ax_recv.at[r * 3 + i, k], device(dx=d))
-                cp.start()
-                sent.append(cp)
-
-    def a_relay(r):
-        for i in range(3):
-            for k, d in enumerate((1, -1)):
-                origin = _rem(x - d, NX)
-                arrival(at.at[r, origin, c, :, columns(i)], ax_recv.at[r * 3 + i, k]).wait_recv()
-                piece = at.at[r, origin, c, pl.ds(k * (share // 2), share // 2), columns(i)]
-                cp = remote(piece, piece, ax_send.at[r * 3 + i, 2 + k], ax_recv.at[r * 3 + i, 2 + k], device(dx=d))
-                cp.start()
-                sent.append(cp)
+    def a_share(r, i):
+        piece = at.at[r, x, c, :, columns(i)]
+        arrival(piece, az_recv.at[r * 3 + i]).wait_recv()
+        for k, d in enumerate((1, -1, 2) if r in X_DIRECT else (1, -1)):
+            cp = remote(piece, piece, ax_send.at[r * 3 + i, k], ax_recv.at[r * 3 + i, k], device(dx=d))
+            cp.start()
+            sent.append(cp)
+
+    def a_relay(r, i):
+        for k, d in enumerate((1, -1)):
+            origin = _rem(x - d, NX)
+            arrival(at.at[r, origin, c, :, columns(i)], ax_recv.at[r * 3 + i, k]).wait_recv()
+            if r in X_DIRECT:
+                continue
+            piece = at.at[r, origin, c, pl.ds(k * (share // 2), share // 2), columns(i)]
+            cp = remote(piece, piece, ax_send.at[r * 3 + i, 2 + k], ax_recv.at[r * 3 + i, 2 + k], device(dx=d))
+            cp.start()
+            sent.append(cp)
 
     def a_core(r):
         origin = _rem(x + 2, NX)
         for i in range(3):
+            if r in X_DIRECT:
+                arrival(at.at[r, origin, c, :, columns(i)], ax_recv.at[r * 3 + i, 2]).wait_recv()
+                continue
             for k in range(2):
                 piece = at.at[r, origin, c, pl.ds(k * (share // 2), share // 2), columns(i)]
                 arrival(piece, ax_recv.at[r * 3 + i, 2 + k]).wait_recv()
@@ -175,51 +177,47 @@
     def a_wait(r):
         arrival(at.at[r, :, 1 - c, :, pl.ds(tok, 3 * tok)], ac_recv.at[r]).wait_recv()
 
-    def first(j):
-        return device(dz=near) if Z_FIRST[j] else device(dy=back_y)
-
-    def second(j):
-        return device(dy=back_y) if Z_FIRST[j] else device(dz=near)
-
-    def p_copy(j, k, to):
+    top, low = pl.ds(0, SPLIT), pl.ds(SPLIT, blk - SPLIT)
+    count = (SPLIT, blk - SPLIT)
+    z_peer, y_peer = device(dz=near), device(dy=back_y)
+
+    def p_copy(j, k, src, dst, to):
+        cp = remote(src, dst, p_send.at[j, k], p_recv.at[j, k], to)
+        cp.start()
+        sent.append(cp)
+
+    def product(j, r):
         cols = pl.ds(0, WIDTHS[j])
-        cp = remote(part.at[j, k, :, cols], land.at[j, k, :, cols], p_send.at[j, k], p_recv.at[j, k], to)
-        cp.start()
-        sent.append(cp)
-
-    def p_wait(j, k):
-        arrival(land.at[j, k, :, pl.ds(0, WIDTHS[j])], p_recv.at[j, k]).wait_recv()
-
-    def product(j, r):
-        wd = WIDTHS[j]
-        value = jnp.dot(at[r].reshape(blk, NZ * tok), gall[j, :, 0:wd], preferred_element_type=F32)
-        if j in DIRECT and r > 0:
-            part[j, r - 1, :, 0:wd] = value.astype(BF16)
-            p_copy(j, r - 1, device(dz=near * (r % 2), dy=back_y * (r // 2)))
-        elif r == 0:
-            own_part[j % OWN, :, 0:wd] = value
-        elif r == (2 if Z_FIRST[j] else 1):
-            kept[j % KEPT, :, 0:wd] = value
+        value = jnp.dot(at[r].reshape(blk, NZ * tok), gall[j, :, cols], preferred_element_type=F32)
+        if r == 0:
+            own_part[j, :, cols] = value
+        elif r == 3:
+            part[j, 2, :, cols] = value.astype(BF16)
+            p_copy(j, 0, part.at[j, 2, top, cols], fwd.at[j, 0, top, cols], y_peer)
+            p_copy(j, 1, part.at[j, 2, low, cols], fwd.at[j, 1, pl.ds(0, blk - SPLIT), cols], z_peer)
+        elif r == 2:
+            part[j, 1, top, cols] = value[:SPLIT].astype(BF16)
+            kept[j, 1, 0:blk - SPLIT, cols] = value[SPLIT:]
+            p_copy(j, 2, part.at[j, 1, top, cols], land.at[j, 1, top, cols], y_peer)
         else:
-            k = 0 if r == 3 else 1
-            part[j, k, :, 0:wd] = value.astype(BF16)
-            p_copy(j, k, first(j))
-
-    def p_pass(j):
-        wd = WIDTHS[j]
-        p_wait(j, 0)
-        part[j, 2, :, 0:wd] = (kept[j % KEPT, :, 0:wd] + land[j, 0, :, 0:wd].astype(F32)).astype(BF16)
-        p_copy(j, 2, second(j))
+            part[j, 0, low, cols] = value[SPLIT:].astype(BF16)
+            kept[j, 0, top, cols] = value[:SPLIT]
+            p_copy(j, 3, part.at[j, 0, low, cols], land.at[j, 0, low, cols], z_peer)
+
+    def p_pass(j, k):
+        cols = pl.ds(0, WIDTHS[j])
+        rows, to = ((top, z_peer), (low, y_peer))[k]
+        held = pl.ds(0, count[k])
+        arrival(fwd.at[j, k, held, cols], p_recv.at[j, k]).wait_recv()
+        part[j, k, rows, cols] = (kept[j, k, held, cols] + fwd[j, k, held, cols].astype(F32)).astype(BF16)
+        p_copy(j, 4 + k, part.at[j, k, rows, cols], land.at[j, k, rows, cols], to)
 
     def finish(j):
         wd = WIDTHS[j]
-        p_wait(j, 1)
-        p_wait(j, 2)
-        total = own_part[j % OWN, :, 0:wd]
-        if j in DIRECT:
-            p_wait(j, 0)
-            total = total + land[j, 0, :, 0:wd].astype(F32)
-        total = total + land[j, 1, :, 0:wd].astype(F32) + land[j, 2, :, 0:wd].astype(F32)
+        cols = pl.ds(0, wd)
+        for k, side, rows in ((2, 1, top), (3, 0, low), (4, 0, top), (5, 1, low)):
+            arrival(land.at[j, side, rows, cols], p_recv.at[j, k]).wait_recv()
+        total = own_part[j, :, cols] + land[j, 0, :, cols].astype(F32) + land[j, 1, :, cols].astype(F32)
         red[:, STARTS[j]:STARTS[j] + wd] = total.astype(BF16)
         half = red[:, STARTS[j]:STARTS[j] + wd]
         for i in range(blk // TILE):
@@ -245,96 +243,120 @@
     a_send(0)
     g_own(0)
     g_own(1)
-    g_own(2)
-    g_own(3)
     turn_own(3)
     turn_own(2)
     turn_own(1)
+    a_share(3, 1)
     turn_own(0)
-    a_share(3)
-    a_share(2)
-    a_share(1)
-    a_relay(3)
-    a_share(0)
-    a_relay(2)
+    a_share(3, 0)
+    a_share(2, 1)
+    a_share(3, 2)
+    a_share(2, 0)
+    a_share(1, 1)
+    a_relay(3, 1)
+    a_share(2, 2)
+    a_share(1, 0)
+    a_relay(3, 0)
+    a_relay(2, 1)
+    a_share(1, 2)
+    a_relay(3, 2)
+    a_relay(2, 0)
+    a_relay(1, 1)
+    a_relay(2, 2)
+    a_share(0, 0)
+    a_share(0, 1)
+    a_share(0, 2)
+    a_relay(1, 0)
     g_pass(0)
-    g_own(4)
-    a_relay(1)
+    g_own(2)
+    a_relay(1, 2)
     a_core(3)
+    a_core(2)
     g_pass(1)
-    g_own(5)
+    g_own(3)
+    a_relay(0, 0)
     g_rest(0)
     a_wait(3)
     product(0, 3)
-    a_relay(0)
+    a_relay(0, 1)
+    a_wait(2)
+    product(0, 2)
+    a_relay(0, 2)
+    a_core(1)
     g_pass(2)
-    g_own(6)
-    a_core(2)
+    g_own(4)
     g_rest(1)
     product(1, 3)
-    a_core(1)
-    a_wait(2)
-    product(0, 2)
     product(1, 2)
-    a_core(0)
-    g_pass(3)
-    g_own(7)
+    p_pass(0, 1)
     a_wait(1)
     product(0, 1)
-    p_pass(0)
+    a_core(0)
+    p_pass(0, 0)
     product(1, 1)
+    g_pass(3)
+    g_own(5)
+    a_wait(0)
+    product(0, 0)
+    product(1, 0)
     g_rest(2)
     product(2, 3)
     product(2, 2)
+    p_pass(1, 1)
+    p_pass(1, 0)
     product(2, 1)
-    a_wait(0)
-    product(0, 0)
-    product(1, 0)
-    p_pass(1)
     product(2, 0)
     g_pass(4)
+    g_own(6)
+    finish(0)
     g_rest(3)
     product(3, 3)
+    product(3, 2)
     product(3, 1)
-    product(3, 2)
     product(3, 0)
-    p_pass(2)
-    finish(0)
+    p_pass(2, 0)
+    p_pass(2, 1)
     g_pass(5)
+    g_own(7)
     g_rest(4)
     product(4, 3)
     product(4, 2)
     product(4, 1)
+    finish(1)
     product(4, 0)
-    finish(1)
+    p_pass(3, 0)
     g_pass(6)
+    p_pass(3, 1)
     g_rest(5)
     product(5, 3)
     product(5, 2)
-    p_pass(3)
     product(5, 1)
     product(5, 0)
-    p_pass(4)
+    finish(2)
+    p_pass(4, 0)
     g_pass(7)
     g_rest(6)
     product(6, 3)
+    product(6, 2)
+    p_pass(4, 1)
     product(6, 1)
-    product(6, 2)
     product(6, 0)
-    finish(2)
-    p_pass(5)
+    p_pass(5, 0)
+    finish(3)
     g_rest(7)
     product(7, 3)
+    p_pass(5, 1)
     product(7, 2)
     product(7, 1)
     product(7, 0)
+    p_pass(6, 0)
+    p_pass(6, 1)
     finish(4)
-    p_pass(6)
-    finish(3)
-    p_pass(7)
+    p_pass(7, 1)
+    p_pass(7, 0)
     finish(5)
+    finish(6)
     finish(7)
-    finish(6)
 
     half_rows = gram.shape[0] // 2
     piece = half_rows // NX
@@ -405,9 +427,10 @@
             pltpu.VMEM((NY, NX, NC, row // NC, NZ * tok), BF16),
             pltpu.VMEM((n, NZ * tok, wide), BF16),
             pltpu.VMEM((n, 3, blk, wide), BF16),
-            pltpu.VMEM((n, 3, blk, wide), BF16),
-            pltpu.VMEM((KEPT, blk, wide), F32),
-            pltpu.VMEM((OWN, blk, wide), F32),
+            pltpu.VMEM((n, 2, SPLIT, wide), BF16),
+            pltpu.VMEM((n, 2, blk, wide), BF16),
+            pltpu.VMEM((n, 2, SPLIT, wide), F32),
+            pltpu.VMEM((n, blk, wide), F32),
             pltpu.VMEM((packed, TILE), F32),
             pltpu.VMEM((packed, TILE), BF16),
             pltpu.VMEM((packed, TILE), BF16),
@@ -417,7 +440,7 @@
             pltpu.VMEM((packed // 8, TILE), BF16),
             pltpu.VMEM((packed // 8, TILE), BF16),
             dma((16 + n,)), dma((12,)), dma((12,)), dma((12, 4)), dma((12, 4)), dma((NY,)), dma((NY,)),
-            dma((n, 4)), dma((n, 4)), dma((n, 3)), dma((n, 3)), dma((9,)), dma((9,)),
+            dma((n, 4)), dma((n, 4)), dma((n, 6)), dma((n, 6)), dma((9,)), dma((9,)),
         ],
         compiler_params=pltpu.CompilerParams(
             collective_id=0, has_side_effects=True, vmem_limit_bytes=56 * 2**20
@@ -431,7 +454,7 @@
     return jnp.dot(a.astype(BF16), b.astype(BF16), preferred_element_type=F32)
 
 
-def root_kernel(refresh, gram, left, old, red, stats, roots, update, state, root, square):
+def root_kernel(refresh, gram, left, old, red, stats, roots, update, state, root, square, pair):
     blk = left.shape[0]
     me = lax.axis_index("dp")
     for k, (i, j) in enumerate(PAIRS):
@@ -454,14 +477,23 @@
             lax.broadcasted_iota(jnp.int32, (blk, blk), 0) == lax.broadcasted_iota(jnp.int32, (blk, blk), 1)
         ).astype(F32)
         root[...] = scale * (1.25 * eye - state[...])
+        pair[0:blk] = state[...].astype(BF16)
         for i in range(ITERS - 1):
-            half = state[...].astype(BF16)
-            square[...] = jnp.dot(half, half, preferred_element_type=F32)
+            half = pair[0:blk]
+            if i == 0:
+                square[...] = jnp.dot(half, half, preferred_element_type=F32)
+            else:
+                pair[blk:] = root[...].astype(BF16)
+                both = jnp.dot(pair[...], half, preferred_element_type=F32)
+                square[...] = both[0:blk]
+                root[...] = 1.25 * root[...] - both[blk:]
             cube = jnp.dot(half, square[...].astype(BF16), preferred_element_type=F32)
             cube = 9.375 * state[...] - 5.0 * square[...] + cube
             last = _mm(square[...], cube)
-            state[...] = 2.44140625 * state[...] - 7.8125 * square[...] + last
-            root[...] = 1.25 * root[...] - _mm(root[...], state[...])
+            value = 2.44140625 * state[...] - 7.8125 * square[...] + last
+            state[...] = value
+            pair[0:blk] = value.astype(BF16)
+        root[...] = 1.25 * root[...] - _mm(root[...], pair[0:blk])
         roots[...] = root[...]
 
     @pl.when(jnp.logical_not(picked))
@@ -483,7 +515,7 @@
         ),
         in_specs=[pl.BlockSpec(memory_space=pltpu.SMEM)] + [vmem] * 4,
         out_specs=[vmem] * 3,
-        scratch_shapes=[pltpu.VMEM((blk, blk), F32)] * 3,
+        scratch_shapes=[pltpu.VMEM((blk, blk), F32)] * 3 + [pltpu.VMEM((2 * blk, blk), BF16)],
         compiler_params=pltpu.CompilerParams(vmem_limit_bytes=40 * 2**20),
         name="root",
     )(refresh, gram, left, old, red)

time: 111 us -> 106 us (0.955); the launches traced: 109 us -> 106 us
  Pallas kernels: 109 us -> 105 us
    pallas_call x1, Pallas kernels: 98.8 us -> 95.6 us  [gradient_call(): pl.pallas_call(gradient_kernel, out_shape=(pltpu.VMEM((blk, ff), BF16), p...]
where the time goes in v3:
time: 106 us
  Pallas kernels  105 us (99%)
    pallas_call x1, Pallas kernels, gradient_call(): pl.pallas_call(gradient_kernel, out_shape=(pltpu.VMEM((blk, ff), BF16), p...  95.6 us
    pallas_call x1, Pallas kernels, root_call(): pl.pallas_call(root_kernel, out_shape=(jax.ShapeDtypeStruct((blk, blk), F...  9.74 us

profile of v3, /device:TPU:1, one launch (start us, length us, event | category | flops | bytes accessed | tf_op | source)
XLA Modules:
  0.0 106.1 jit_solution(16545894015325003700)
XLA Ops:
  0.6 0.0 copy-start.2
  0.6 0.0 copy-start.1
  0.7 0.0 copy-start
  0.7 95.6 %gradient.1 = (bf16[512,1024]{1,0:T(8,128)(2,1)S(1)}, bf16[1280,128]{1,0:T(8,128)(2,1)S(1)}) custom-call(bf16[384,8192]{1,0:T(8,128)(2,1)} %act.1, bf16[384,1024]{1,0:T(8,128)(2,1)} %grad.1), custom_call_target="tpu_custom_call" | custom-call | flops 6979321856 | bytes 8388608 | tf_op jit(solution)/shard_map/gradient/pallas_call | solution.py:418
  96.3 0.0 copy-done.2
  96.3 0.0 copy-done.1
  96.3 0.0 copy-done
  96.3 9.7 %root.1 = (f32[512,512]{1,0:T(8,128)}, f32[512,512]{1,0:T(8,128)}, bf16[512,1024]{1,0:T(8,128)(2,1)}) custom-call(s32[4]{0:T(128)S(1)} %copy-done.2, bf16[1280,128]{1,0:T(8,128)(2,1)S(1)} %get-tuple-element.5.gram, f32[512,512]{1,0:T(8,128)S(1)} %copy-done, f32[512,512]{1,0:T(8,128)S(1)} %copy-done.1, bf16[512,1024]{1,0:T(8,128)(2,1)S(1)} %get-tuple-element.6.red), custom_call_target="tpu_custom_call" | custom-call | tf_op jit(solution)/shard_map/root/pallas_call | solution.py:509
Async XLA Ops:
  0.6 95.7 %copy-start.2 = (s32[4]{0:T(128)S(1)}, s32[4]{0:T(128)}, u32[]{:S(2)}) copy-start(s32[4]{0:T(128)} %refresh.1) | copy-start | bytes 52
  0.6 95.7 %copy-start.1 = (f32[512,512]{1,0:T(8,128)S(1)}, f32[512,512]{1,0:T(8,128)}, u32[]{:S(2)}) copy-start(f32[512,512]{1,0:T(8,128)} %old.1) | copy-start | bytes 3145732
  0.7 95.7 %copy-start = (f32[512,512]{1,0:T(8,128)S(1)}, f32[512,512]{1,0:T(8,128)}, u32[]{:S(2)}) copy-start(f32[512,512]{1,0:T(8,128)} %left.1) | copy-start | bytes 3145732

commit v4 on v3

--- a/solution.py
+++ b/solution.py
@@ -14,7 +14,7 @@
 MESH = pl.DeviceIdType.MESH
 WIDTHS = (128, 128, 128, 128, 128, 128, 128, 128)
 STARTS = tuple(sum(WIDTHS[:i]) for i in range(len(WIDTHS)))
-SPLIT = 384
+SPLIT = (384, 384, 384, 384, 384, 256, 256, 256)
 X_DIRECT = ()
 ORDER = (3, 2, 1, 0)
 TILE = 128
@@ -57,8 +57,8 @@
     def arrival(dst, recv):
         return remote(dst, dst, recv, recv, device(dc=1))
 
-    far = jnp.where(c == 0, 2, -2)
     line = jnp.where(zl < 2, 2, -2)
+    far = -line
     near = 1 - 2 * lax.rem(zl, 2)
     even_y = 1 - 2 * lax.rem(y, 2)
     back_y = NY - 1 - 2 * y
@@ -177,8 +177,6 @@
     def a_wait(r):
         arrival(at.at[r, :, 1 - c, :, pl.ds(tok, 3 * tok)], ac_recv.at[r]).wait_recv()
 
-    top, low = pl.ds(0, SPLIT), pl.ds(SPLIT, blk - SPLIT)
-    count = (SPLIT, blk - SPLIT)
     z_peer, y_peer = device(dz=near), device(dy=back_y)
 
     def p_copy(j, k, src, dst, to):
@@ -186,28 +184,32 @@
         cp.start()
         sent.append(cp)
 
+    def parts(j):
+        return pl.ds(0, SPLIT[j]), pl.ds(SPLIT[j], blk - SPLIT[j])
+
     def product(j, r):
         cols = pl.ds(0, WIDTHS[j])
+        (top, low), cut = parts(j), SPLIT[j]
         value = jnp.dot(at[r].reshape(blk, NZ * tok), gall[j, :, cols], preferred_element_type=F32)
         if r == 0:
             own_part[j, :, cols] = value
         elif r == 3:
             part[j, 2, :, cols] = value.astype(BF16)
             p_copy(j, 0, part.at[j, 2, top, cols], fwd.at[j, 0, top, cols], y_peer)
-            p_copy(j, 1, part.at[j, 2, low, cols], fwd.at[j, 1, pl.ds(0, blk - SPLIT), cols], z_peer)
+            p_copy(j, 1, part.at[j, 2, low, cols], fwd.at[j, 1, pl.ds(0, blk - cut), cols], z_peer)
         elif r == 2:
-            part[j, 1, top, cols] = value[:SPLIT].astype(BF16)
-            kept[j, 1, 0:blk - SPLIT, cols] = value[SPLIT:]
+            part[j, 1, top, cols] = value[:cut].astype(BF16)
+            kept[j, 1, 0:blk - cut, cols] = value[cut:]
             p_copy(j, 2, part.at[j, 1, top, cols], land.at[j, 1, top, cols], y_peer)
         else:
-            part[j, 0, low, cols] = value[SPLIT:].astype(BF16)
-            kept[j, 0, top, cols] = value[:SPLIT]
+            part[j, 0, low, cols] = value[cut:].astype(BF16)
+            kept[j, 0, top, cols] = value[:cut]
             p_copy(j, 3, part.at[j, 0, low, cols], land.at[j, 0, low, cols], z_peer)
 
     def p_pass(j, k):
         cols = pl.ds(0, WIDTHS[j])
-        rows, to = ((top, z_peer), (low, y_peer))[k]
-        held = pl.ds(0, count[k])
+        rows, to = (parts(j)[k], (z_peer, y_peer)[k])
+        held = pl.ds(0, (SPLIT[j], blk - SPLIT[j])[k])
         arrival(fwd.at[j, k, held, cols], p_recv.at[j, k]).wait_recv()
         part[j, k, rows, cols] = (kept[j, k, held, cols] + fwd[j, k, held, cols].astype(F32)).astype(BF16)
         p_copy(j, 4 + k, part.at[j, k, rows, cols], land.at[j, k, rows, cols], to)
@@ -215,6 +217,7 @@
     def finish(j):
         wd = WIDTHS[j]
         cols = pl.ds(0, wd)
+        top, low = parts(j)
         for k, side, rows in ((2, 1, top), (3, 0, low), (4, 0, top), (5, 1, low)):
             arrival(land.at[j, side, rows, cols], p_recv.at[j, k]).wait_recv()
         total = own_part[j, :, cols] + land[j, 0, :, cols].astype(F32) + land[j, 1, :, cols].astype(F32)
@@ -237,123 +240,123 @@
         at[r, :, :, :, 0:tok] = raw_own[r].T.reshape(NX, NC, share, tok)
 
     n = len(WIDTHS)
+    g_own(0)
+    g_own(1)
     a_send(3)
     a_send(2)
     a_send(1)
-    a_send(0)
-    g_own(0)
-    g_own(1)
     turn_own(3)
     turn_own(2)
     turn_own(1)
-    a_share(3, 1)
     turn_own(0)
     a_share(3, 0)
-    a_share(2, 1)
-    a_share(3, 2)
-    a_share(2, 0)
-    a_share(1, 1)
-    a_relay(3, 1)
-    a_share(2, 2)
-    a_share(1, 0)
-    a_relay(3, 0)
-    a_relay(2, 1)
-    a_share(1, 2)
-    a_relay(3, 2)
-    a_relay(2, 0)
-    a_relay(1, 1)
-    a_relay(2, 2)
-    a_share(0, 0)
-    a_share(0, 1)
-    a_share(0, 2)
-    a_relay(1, 0)
+    a_share(3, 1)
     g_pass(0)
     g_own(2)
-    a_relay(1, 2)
-    a_core(3)
-    a_core(2)
+    a_share(3, 2)
+    a_relay(3, 0)
+    a_share(2, 1)
+    a_share(2, 0)
+    a_relay(3, 1)
     g_pass(1)
     g_own(3)
-    a_relay(0, 0)
+    a_share(2, 2)
+    a_relay(3, 2)
+    a_share(1, 1)
+    a_share(1, 0)
+    a_relay(2, 1)
+    g_pass(2)
+    g_own(4)
+    a_relay(2, 0)
+    a_share(1, 2)
+    a_relay(2, 2)
+    a_core(3)
+    a_relay(1, 1)
+    g_pass(3)
+    g_own(5)
+    a_send(0)
+    a_relay(1, 0)
     g_rest(0)
     a_wait(3)
     product(0, 3)
-    a_relay(0, 1)
+    g_rest(1)
+    product(1, 3)
+    a_relay(1, 2)
+    a_core(2)
+    g_pass(4)
+    g_own(6)
     a_wait(2)
     product(0, 2)
-    a_relay(0, 2)
     a_core(1)
-    g_pass(2)
-    g_own(4)
-    g_rest(1)
-    product(1, 3)
     product(1, 2)
+    g_rest(2)
+    product(2, 3)
+    a_share(0, 0)
+    product(2, 2)
     p_pass(0, 1)
     a_wait(1)
     product(0, 1)
+    g_pass(5)
+    g_own(7)
+    product(1, 1)
+    product(2, 1)
+    p_pass(0, 0)
+    p_pass(1, 0)
+    p_pass(1, 1)
+    g_rest(3)
+    product(3, 3)
+    a_relay(0, 0)
+    p_pass(2, 1)
+    product(3, 1)
+    product(3, 2)
+    g_pass(6)
+    a_share(0, 1)
+    p_pass(2, 0)
+    a_share(0, 2)
+    g_rest(4)
+    product(4, 3)
+    g_pass(7)
+    a_relay(0, 1)
+    product(4, 1)
+    product(4, 2)
+    a_relay(0, 2)
+    p_pass(3, 0)
+    p_pass(3, 1)
+    g_rest(5)
+    product(5, 3)
+    product(5, 1)
+    product(5, 2)
     a_core(0)
-    p_pass(0, 0)
-    product(1, 1)
-    g_pass(3)
-    g_own(5)
+    p_pass(4, 1)
+    p_pass(4, 0)
+    g_rest(6)
+    product(6, 3)
+    product(6, 1)
+    product(6, 2)
     a_wait(0)
     product(0, 0)
     product(1, 0)
-    g_rest(2)
-    product(2, 3)
-    product(2, 2)
-    p_pass(1, 1)
-    p_pass(1, 0)
-    product(2, 1)
-    product(2, 0)
-    g_pass(4)
-    g_own(6)
-    finish(0)
-    g_rest(3)
-    product(3, 3)
-    product(3, 2)
-    product(3, 1)
-    product(3, 0)
-    p_pass(2, 0)
-    p_pass(2, 1)
-    g_pass(5)
-    g_own(7)
-    g_rest(4)
-    product(4, 3)
-    product(4, 2)
-    product(4, 1)
-    finish(1)
-    product(4, 0)
-    p_pass(3, 0)
-    g_pass(6)
-    p_pass(3, 1)
-    g_rest(5)
-    product(5, 3)
-    product(5, 2)
-    product(5, 1)
-    product(5, 0)
-    finish(2)
-    p_pass(4, 0)
-    g_pass(7)
-    g_rest(6)
-    product(6, 3)
-    product(6, 2)
-    p_pass(4, 1)
-    product(6, 1)
-    product(6, 0)
-    p_pass(5, 0)
-    finish(3)
     g_rest(7)
     product(7, 3)
+    product(7, 1)
     p_pass(5, 1)
     product(7, 2)
-    product(7, 1)
+    product(2, 0)
+    product(3, 0)
+    p_pass(5, 0)
+    product(4, 0)
+    finish(0)
+    product(5, 0)
+    finish(1)
+    product(6, 0)
+    finish(2)
     product(7, 0)
+    finish(3)
+    finish(4)
     p_pass(6, 0)
     p_pass(6, 1)
-    finish(4)
+    p_pass(7, 0)
     p_pass(7, 1)
-    p_pass(7, 0)
     finish(5)
     finish(6)
     finish(7)
@@ -427,9 +430,9 @@
             pltpu.VMEM((NY, NX, NC, row // NC, NZ * tok), BF16),
             pltpu.VMEM((n, NZ * tok, wide), BF16),
             pltpu.VMEM((n, 3, blk, wide), BF16),
-            pltpu.VMEM((n, 2, SPLIT, wide), BF16),
+            pltpu.VMEM((n, 2, max(SPLIT), wide), BF16),
             pltpu.VMEM((n, 2, blk, wide), BF16),
-            pltpu.VMEM((n, 2, SPLIT, wide), F32),
+            pltpu.VMEM((n, 2, max(SPLIT), wide), F32),
             pltpu.VMEM((n, blk, wide), F32),
             pltpu.VMEM((packed, TILE), F32),
             pltpu.VMEM((packed, TILE), BF16),

time: 106 us -> 102 us (0.962)
  Pallas kernels: 105 us -> 102 us
    pallas_call x1, Pallas kernels: 95.6 us -> 91.9 us  [gradient_call(): pl.pallas_call(gradient_kernel, out_shape=(pltpu.VMEM((blk, ff), BF16), p...]
where the time goes in v4:
time: 102 us
  Pallas kernels  102 us (100%)
    pallas_call x1, Pallas kernels, gradient_call(): pl.pallas_call(gradient_kernel, out_shape=(pltpu.VMEM((blk, ff), BF16), p...  91.9 us
    pallas_call x1, Pallas kernels, root_call(): pl.pallas_call(root_kernel, out_shape=(jax.ShapeDtypeStruct((blk, blk), F...  9.74 us

profile of v4, /device:TPU:1, one launch (start us, length us, event | category | flops | bytes accessed | tf_op | source)
XLA Modules:
  0.0 102.3 jit_solution(14234321662389290083)
XLA Ops:
  0.6 0.0 copy-start.2
  0.6 0.0 copy-start.1
  0.7 0.0 copy-start
  0.7 91.9 %gradient.1 = (bf16[512,1024]{1,0:T(8,128)(2,1)S(1)}, bf16[1280,128]{1,0:T(8,128)(2,1)S(1)}) custom-call(bf16[384,8192]{1,0:T(8,128)(2,1)} %act.1, bf16[384,1024]{1,0:T(8,128)(2,1)} %grad.1), custom_call_target="tpu_custom_call" | custom-call | flops 6979321856 | bytes 8388608 | tf_op jit(solution)/shard_map/gradient/pallas_call | solution.py:421
  92.5 0.0 copy-done.2
  92.5 0.0 copy-done.1
  92.6 0.0 copy-done
  92.6 9.7 %root.1 = (f32[512,512]{1,0:T(8,128)}, f32[512,512]{1,0:T(8,128)}, bf16[512,1024]{1,0:T(8,128)(2,1)}) custom-call(s32[4]{0:T(128)S(1)} %copy-done.2, bf16[1280,128]{1,0:T(8,128)(2,1)S(1)} %get-tuple-element.5.gram, f32[512,512]{1,0:T(8,128)S(1)} %copy-done, f32[512,512]{1,0:T(8,128)S(1)} %copy-done.1, bf16[512,1024]{1,0:T(8,128)(2,1)S(1)} %get-tuple-element.6.red), custom_call_target="tpu_custom_call" | custom-call | tf_op jit(solution)/shard_map/root/pallas_call | solution.py:512
Async XLA Ops:
  0.6 91.9 %copy-start.2 = (s32[4]{0:T(128)S(1)}, s32[4]{0:T(128)}, u32[]{:S(2)}) copy-start(s32[4]{0:T(128)} %refresh.1) | copy-start | bytes 52
  0.6 91.9 %copy-start.1 = (f32[512,512]{1,0:T(8,128)S(1)}, f32[512,512]{1,0:T(8,128)}, u32[]{:S(2)}) copy-start(f32[512,512]{1,0:T(8,128)} %old.1) | copy-start | bytes 3145732
  0.7 91.9 %copy-start = (f32[512,512]{1,0:T(8,128)S(1)}, f32[512,512]{1,0:T(8,128)}, u32[]{:S(2)}) copy-start(f32[512,512]{1,0:T(8,128)} %left.1) | copy-start | bytes 3145732

commit v5 on v4

--- a/solution.py
+++ b/solution.py
@@ -396,15 +396,19 @@
         cp = remote(final, final, m_send.at[5 + k], m_recv.at[5 + k], device(dx=d))
         cp.start()
         sent.append(cp)
-    for k, d in enumerate((2, 1, 3)):
-        rows = pl.multiple_of(c * half_rows + _rem(x - d, NX) * piece, 32)
-        arrival(gram_half.at[pl.ds(rows, piece)], m_recv.at[5 + k]).wait_recv()
-    mine_half = gram_half.at[pl.ds(pl.multiple_of(c * half_rows, 128), half_rows)]
-    cp = remote(mine_half, mine_half, m_send.at[8], m_recv.at[8], device(dc=1))
+    cp = remote(final, final, m_send.at[8], m_recv.at[8], device(dc=1))
     cp.start()
     sent.append(cp)
-    arrival(gram_half.at[pl.ds(pl.multiple_of((1 - c) * half_rows, 128), half_rows)], m_recv.at[8]).wait_recv()
-
+    for k, d in ((1, 1), (2, 3), (0, 2)):
+        rows = pl.multiple_of(c * half_rows + _rem(x - d, NX) * piece, 32)
+        slot = gram_half.at[pl.ds(rows, piece)]
+        arrival(slot, m_recv.at[5 + k]).wait_recv()
+        cp = remote(slot, slot, m_send.at[9 + k], m_recv.at[9 + k], device(dc=1))
+        cp.start()
+        sent.append(cp)
+    for k, d in ((-1, 0), (1, 1), (2, 3), (0, 2)):
+        rows = pl.multiple_of((1 - c) * half_rows + _rem(x - d, NX) * piece, 32)
+        arrival(gram_half.at[pl.ds(rows, piece)], m_recv.at[9 + k]).wait_recv()
     gram_out[...] = gram_half[...]
 
     for cp in sent:
@@ -443,7 +447,7 @@
             pltpu.VMEM((packed // 8, TILE), BF16),
             pltpu.VMEM((packed // 8, TILE), BF16),
             dma((16 + n,)), dma((12,)), dma((12,)), dma((12, 4)), dma((12, 4)), dma((NY,)), dma((NY,)),
-            dma((n, 4)), dma((n, 4)), dma((n, 6)), dma((n, 6)), dma((9,)), dma((9,)),
+            dma((n, 4)), dma((n, 4)), dma((n, 6)), dma((n, 6)), dma((12,)), dma((12,)),
         ],
         compiler_params=pltpu.CompilerParams(
             collective_id=0, has_side_effects=True, vmem_limit_bytes=56 * 2**20

time: 102 us -> 102 us (level)
  no operation moved by 1% of the time
where the time goes in v5:
time: 102 us
  Pallas kernels  102 us (100%)
    pallas_call x1, Pallas kernels, gradient_call(): pl.pallas_call(gradient_kernel, out_shape=(pltpu.VMEM((blk, ff), BF16), p...  91.9 us
    pallas_call x1, Pallas kernels, root_call(): pl.pallas_call(root_kernel, out_shape=(jax.ShapeDtypeStruct((blk, blk), F...  9.74 us

profile of v5, /device:TPU:1, one launch (start us, length us, event | category | flops | bytes accessed | tf_op | source)
XLA Modules:
  0.0 102.3 jit_solution(16524537174443419034)
XLA Ops:
  0.6 0.0 copy-start.2
  0.6 0.0 copy-start.1
  0.7 0.0 copy-start
  0.7 91.9 %gradient.1 = (bf16[512,1024]{1,0:T(8,128)(2,1)S(1)}, bf16[1280,128]{1,0:T(8,128)(2,1)S(1)}) custom-call(bf16[384,8192]{1,0:T(8,128)(2,1)} %act.1, bf16[384,1024]{1,0:T(8,128)(2,1)} %grad.1), custom_call_target="tpu_custom_call" | custom-call | flops 6979321856 | bytes 8388608 | tf_op jit(solution)/shard_map/gradient/pallas_call | solution.py:425
  92.5 0.0 copy-done.2
  92.5 0.0 copy-done.1
  92.5 0.0 copy-done
  92.6 9.7 %root.1 = (f32[512,512]{1,0:T(8,128)}, f32[512,512]{1,0:T(8,128)}, bf16[512,1024]{1,0:T(8,128)(2,1)}) custom-call(s32[4]{0:T(128)S(1)} %copy-done.2, bf16[1280,128]{1,0:T(8,128)(2,1)S(1)} %get-tuple-element.5.gram, f32[512,512]{1,0:T(8,128)S(1)} %copy-done, f32[512,512]{1,0:T(8,128)S(1)} %copy-done.1, bf16[512,1024]{1,0:T(8,128)(2,1)S(1)} %get-tuple-element.6.red), custom_call_target="tpu_custom_call" | custom-call | tf_op jit(solution)/shard_map/root/pallas_call | solution.py:516
Async XLA Ops:
  0.6 91.9 %copy-start.2 = (s32[4]{0:T(128)S(1)}, s32[4]{0:T(128)}, u32[]{:S(2)}) copy-start(s32[4]{0:T(128)} %refresh.1) | copy-start | bytes 52
  0.6 91.9 %copy-start.1 = (f32[512,512]{1,0:T(8,128)S(1)}, f32[512,512]{1,0:T(8,128)}, u32[]{:S(2)}) copy-start(f32[512,512]{1,0:T(8,128)} %old.1) | copy-start | bytes 3145732
  0.7 91.9 %copy-start = (f32[512,512]{1,0:T(8,128)S(1)}, f32[512,512]{1,0:T(8,128)}, u32[]{:S(2)}) copy-start(f32[512,512]{1,0:T(8,128)} %left.1) | copy-start | bytes 3145732
